TPU v7x, 256 devices: a whole 4x4x8 slice. The times are simulated.
256 devices in a mesh: dp: 8 (over z), cent: 32 (over y, x, core).
Axes of the slice: x: 4, y: 4, z: 8, core: 2. Of those that a mesh axis runs over, the one named last changes fastest.
Arguments:
- embeddings: bfloat16 [16384, 768], P(('dp', 'cent')), may hold values from -8 to 8
- centroids: bfloat16 [65536, 768], P('cent'), may hold values from -3 to 3
Outputs:
- new_centroids: bfloat16 [65536, 768], P('cent')
All inputs are finite; a program needn't handle non-finite values.
Results may differ from a plain program's by a relative error of at most 0.0038.
Values may be sent and summed in bfloat16 or wider, within the bound.
No kernel may reach another device: no remote copies, remote signals or barrier semaphores. Data moves between devices by JAX's collectives and lax.ppermute only.
A program may use at most 128 MiB of HBM per device.

v0:
```python
import math

import jax
import jax.numpy as jnp
from jax import lax
from jax.sharding import PartitionSpec as P

ITERS = 2


def row_norm(logits, col_pot):
    shifted = logits + col_pot[None, :]
    peak = lax.pmax(jnp.max(shifted, axis=1), "cent")
    total = lax.psum(jnp.sum(jnp.exp(shifted - peak[:, None]), axis=1), "cent")
    return -(peak + jnp.log(total))


def col_norm(logits, row_pot, log_ratio):
    shifted = logits + row_pot[:, None]
    peak = lax.pmax(jnp.max(shifted, axis=0), "dp")
    total = lax.psum(jnp.sum(jnp.exp(shifted - peak[None, :]), axis=0), "dp")
    return log_ratio - (peak + jnp.log(total))


def shards(embeddings, centroids):
    docs = lax.all_gather(embeddings, "cent", axis=0, tiled=True)
    logits = 3.0 * lax.dot_general(
        docs, centroids, (((1,), (1,)), ((), ())), preferred_element_type=jnp.float32
    )
    doc_count = docs.shape[0] * lax.axis_size("dp")
    cent_count = centroids.shape[0] * lax.axis_size("cent")
    log_ratio = math.log(doc_count / cent_count)
    row_pot = jnp.zeros((docs.shape[0],), jnp.float32)
    col_pot = jnp.zeros((centroids.shape[0],), jnp.float32)
    for repeat in range(ITERS):
        col_pot = col_norm(logits, row_pot, log_ratio)
        row_pot = row_norm(logits, col_pot)
    plan = jnp.exp(logits + row_pot[:, None] + col_pot[None, :]).astype(jnp.bfloat16)
    sums = lax.dot_general(plan, docs, (((0,), (0,)), ((), ())), preferred_element_type=jnp.float32)
    ones_column = jnp.ones((plan.shape[0],), jnp.bfloat16)
    mass = jnp.dot(ones_column, plan, preferred_element_type=jnp.float32)
    total_sums, total_mass = lax.psum((sums, mass), "dp")
    return (total_sums / total_mass[:, None]).astype(jnp.bfloat16)


def solution(mesh):
    placed = (P(("dp", "cent"), None), P("cent", None))
    return jax.shard_map(
        shards, mesh=mesh, in_specs=placed, out_specs=P("cent", None), check_vma=False
    )
```

profile of v0, /device:TPU:1, one launch (start us, length us, event | category | flops | bytes accessed | tf_op | source)
XLA Modules:
  0.0 624.4 jit_solution(11902746682201578213)
XLA Ops:
  6.5 0.0 copy-start
  6.5 0.0 all-gather.2.cloned.1.call-start
  6.5 0.7 all-gather.2.cloned.1.call-update
  7.3 0.0 all-reduce.2.cloned.1.call-start
  7.3 56.9 %all-gather.2.cloned.1.call-done = bf16[2048,768]{1,0:T(8,128)(2,1)} async-done(((bf16[64,768]{1,0:T(8,128)(2,1)}), bf16[2048,768]{1,0:T(8,128)(2,1)}) %all-gather.2.cloned.1.call-update) | async-done | bytes 3145744 | tf_op jit(solution)/shard_map/all_gather | solution.py:26
  64.2 0.0 copy-done
  64.2 12.0 %multiply_reduce_fusion = (f32[2048]{0:T(1024)S(1)}, f32[2048,2048]{1,0:T(8,128)}) fusion(bf16[2048,768]{1,0:T(8,128)(2,1)} %all-gather.2.cloned.1.call-done, bf16[2048,768]{1,0:T(8,128)(2,1)S(1)} %copy-done), kind=kOutput, calls=%fused_computation.8 | convolution fusion | flops 6450837504 | bytes 23076864 | tf_op jit(solution)/shard_map/dot_general | solution.py:27
  76.3 14.0 %pmax.28 = f32[2048]{0:T(1024)S(1)} all-reduce(f32[2048]{0:T(1024)S(1)} %get-tuple-element.5), channel_id=1, replica_groups=mesh['dp'=8,'cent'=32] {'dp'}, use_global_device_ids=true, to_apply=%region_1.0 | all-reduce | flops 2048 | bytes 16384 | tf_op jit(solution)/shard_map/pmax | solution.py:20
  90.3 8.5 %exponential_reduce_fusion.3 = f32[2048]{0:T(1024)S(1)} fusion(f32[2048,2048]{1,0:T(8,128)} %get-tuple-element.6, f32[2048]{0:T(1024)S(1)} %pmax.28), kind=kLoop, calls=%fused_computation.4 | loop fusion | flops 12580864 | bytes 16793600 | tf_op jit(solution)/shard_map/reduce_sum | solution.py:21
  98.9 11.4 %psum.42 = f32[2048]{0:T(1024)S(1)} all-reduce(f32[2048]{0:T(1024)S(1)} %exponential_reduce_fusion.3), channel_id=1, replica_groups=mesh['dp'=8,'cent'=32] {'dp'}, use_global_device_ids=true, to_apply=%region_3.0 | all-reduce | flops 2048 | bytes 16384 | tf_op jit(solution)/shard_map/psum | solution.py:21
  110.3 7.5 %add_reduce_fusion.2 = f32[2048]{0:T(1024)S(1)} fusion(f32[2048,2048]{1,0:T(8,128)} %get-tuple-element.6, f32[2048]{0:T(1024)S(1)} %add_subtract_fusion.1), kind=kLoop, calls=%fused_computation.7 | loop fusion | flops 12580864 | bytes 16793600 | tf_op jit(solution)/shard_map/reduce_max | solution.py:13
  117.8 70.8 %pmax.29 = f32[2048]{0:T(1024)S(1)} all-reduce(f32[2048]{0:T(1024)S(1)} %add_reduce_fusion.2), channel_id=1, replica_groups=mesh['dp'=8,'cent'=32] {'cent'}, use_global_device_ids=true, to_apply=%region_5.0 | all-reduce | flops 2048 | bytes 16384 | tf_op jit(solution)/shard_map/pmax | solution.py:13
  188.6 8.0 %exponential_reduce_fusion.2 = f32[2048]{0:T(1024)S(1)} fusion(f32[2048,2048]{1,0:T(8,128)} %get-tuple-element.6, f32[2048]{0:T(1024)S(1)} %pmax.29, f32[2048]{0:T(1024)S(1)} %add_subtract_fusion.1), kind=kLoop, calls=%fused_computation.3 | loop fusion | flops 16775168 | bytes 16801792 | tf_op jit(solution)/shard_map/reduce_sum | solution.py:14
  196.6 63.7 %psum.43 = f32[2048]{0:T(1024)S(1)} all-reduce(f32[2048]{0:T(1024)S(1)} %exponential_reduce_fusion.2), channel_id=1, replica_groups=mesh['dp'=8,'cent'=32] {'cent'}, use_global_device_ids=true, to_apply=%region_7.0 | all-reduce | flops 2048 | bytes 16384 | tf_op jit(solution)/shard_map/psum | solution.py:14
  260.3 7.5 %add_reduce_fusion.1 = f32[2048]{0:T(1024)S(1)} fusion(f32[2048,2048]{1,0:T(8,128)} %get-tuple-element.6, f32[2048]{0:T(1024)S(1)} %add_negate_fusion.1), kind=kLoop, calls=%fused_computation.6 | loop fusion | flops 12580864 | bytes 16793600 | tf_op jit(solution)/shard_map/reduce_max | solution.py:20
  267.8 12.0 %pmax.30 = f32[2048]{0:T(1024)S(1)} all-reduce(f32[2048]{0:T(1024)S(1)} %add_reduce_fusion.1), channel_id=1, replica_groups=mesh['dp'=8,'cent'=32] {'dp'}, use_global_device_ids=true, to_apply=%region_9.0 | all-reduce | flops 2048 | bytes 16384 | tf_op jit(solution)/shard_map/pmax | solution.py:20
  279.7 8.0 %exponential_reduce_fusion.1 = f32[2048]{0:T(1024)S(1)} fusion(f32[2048,2048]{1,0:T(8,128)} %get-tuple-element.6, f32[2048]{0:T(1024)S(1)} %pmax.30, f32[2048]{0:T(1024)S(1)} %add_negate_fusion.1), kind=kLoop, calls=%fused_computation.2 | loop fusion | flops 16775168 | bytes 16801792 | tf_op jit(solution)/shard_map/reduce_sum | solution.py:21
  287.8 12.0 %psum.44 = f32[2048]{0:T(1024)S(1)} all-reduce(f32[2048]{0:T(1024)S(1)} %exponential_reduce_fusion.1), channel_id=1, replica_groups=mesh['dp'=8,'cent'=32] {'dp'}, use_global_device_ids=true, to_apply=%region_11.0 | all-reduce | flops 2048 | bytes 16384 | tf_op jit(solution)/shard_map/psum | solution.py:21
  299.8 7.5 %add_reduce_fusion = f32[2048]{0:T(1024)S(1)} fusion(f32[2048,2048]{1,0:T(8,128)} %get-tuple-element.6, f32[2048]{0:T(1024)S(1)} %add_subtract_fusion), kind=kLoop, calls=%fused_computation.5 | loop fusion | flops 12580864 | bytes 16793600 | tf_op jit(solution)/shard_map/reduce_max | solution.py:13
  307.2 70.8 %pmax.31 = f32[2048]{0:T(1024)S(1)} all-reduce(f32[2048]{0:T(1024)S(1)} %add_reduce_fusion), channel_id=1, replica_groups=mesh['dp'=8,'cent'=32] {'cent'}, use_global_device_ids=true, to_apply=%region_13.0 | all-reduce | flops 2048 | bytes 16384 | tf_op jit(solution)/shard_map/pmax | solution.py:13
  378.0 7.9 %exponential_reduce_fusion = f32[2048]{0:T(1024)S(1)} fusion(f32[2048,2048]{1,0:T(8,128)} %get-tuple-element.6, f32[2048]{0:T(1024)S(1)} %pmax.31, f32[2048]{0:T(1024)S(1)} %add_subtract_fusion), kind=kLoop, calls=%fused_computation.1 | loop fusion | flops 16775168 | bytes 16801792 | tf_op jit(solution)/shard_map/reduce_sum | solution.py:14
  385.9 63.7 %psum.45 = f32[2048]{0:T(1024)S(1)} all-reduce(f32[2048]{0:T(1024)S(1)} %exponential_reduce_fusion), channel_id=1, replica_groups=mesh['dp'=8,'cent'=32] {'cent'}, use_global_device_ids=true, to_apply=%region_15.0 | all-reduce | flops 2048 | bytes 16384 | tf_op jit(solution)/shard_map/psum | solution.py:14
  449.6 0.0 copy-start.2
  449.7 7.9 %exponential_convert_fusion = bf16[2048,2048]{1,0:T(8,128)(2,1)S(1)} fusion(f32[2048,2048]{1,0:T(8,128)} %get-tuple-element.6, f32[2048]{0:T(1024)S(1)} %add_negate_fusion, f32[2048]{0:T(1024)S(1)} %add_subtract_fusion), kind=kLoop, calls=%fused_computation | loop fusion | flops 16777216 | bytes 25182208 | tf_op jit(solution)/shard_map/convert_element_type | solution.py:38
  457.6 0.0 copy-start.1
  457.6 3.2 copy-done.1
  460.8 0.0 copy-done.2
  460.8 8.9 %fusion.3 = f32[2048,768]{1,0:T(8,128)} fusion(bf16[2048,2048]{1,0:T(8,128)(2,1)S(1)} %exponential_convert_fusion, bf16[2048,768]{1,0:T(8,128)(2,1)S(1)} %copy-done.2), kind=kOutput, calls=%fused_computation.17 | convolution fusion | flops 6442450944 | bytes 17825792 | tf_op jit(solution)/shard_map/dot_general | solution.py:39
  469.7 0.0 all-reduce.2.cloned.1.call-update
  469.7 4.6 fusion
  474.3 13.8 %psum.47 = f32[2048]{0:T(1024)S(1)} all-reduce(f32[2048]{0:T(1024)S(1)} %bitcast.6), channel_id=1, replica_groups=mesh['dp'=8,'cent'=32] {'dp'}, use_global_device_ids=true, to_apply=%region_17.0 | all-reduce | flops 2048 | bytes 16384 | tf_op jit(solution)/shard_map/psum | solution.py:42
  488.2 124.5 %all-reduce.2.cloned.1.call-done = f32[2048,768]{1,0:T(8,128)} async-done(((f32[2048,768]{1,0:T(8,128)}), f32[2048,768]{1,0:T(8,128)}) %all-reduce.2.cloned.1.call-update) | async-done | bytes 6291472 | tf_op jit(solution)/shard_map/psum | solution.py:42
  612.7 4.9 divide_convert_fusion
  (4 shorter events, 0.0 us)
Async XLA Ops:
  6.5 57.7 %copy-start = (bf16[2048,768]{1,0:T(8,128)(2,1)S(1)}, bf16[2048,768]{1,0:T(8,128)(2,1)}, u32[]{:S(2)}) copy-start(bf16[2048,768]{1,0:T(8,128)(2,1)} %param.3) | copy-start | bytes 9437188
  6.5 57.7 %all-gather.2.cloned.1.call-start = ((), (), s32[]{:S(2)}) async-start(), calls=%async_computation | async-start | bytes 3244032 | tf_op jit(solution)/shard_map/all_gather | solution.py:26
  7.3 605.4 %all-reduce.2.cloned.1.call-start = ((), (), s32[]{:S(2)}) async-start(), calls=%async_computation.1 | async-start | bytes 12582912 | tf_op jit(solution)/shard_map/psum | solution.py:42
  449.6 11.2 %copy-start.2 = (bf16[2048,768]{1,0:T(8,128)(2,1)S(1)}, bf16[2048,768]{1,0:T(8,128)(2,1)}, u32[]{:S(2)}) copy-start(bf16[2048,768]{1,0:T(8,128)(2,1)} %all-gather.2.cloned.1.call-done) | copy-start | bytes 9437188
  457.6 3.2 copy-start.1
Sparse Core Ops, SparseCore 0:
  9.9 54.2 all-gather.1
  469.9 142.7 all-reduce.1
where the time goes:
time: 625 us; the launch traced here: 624 us
  blocking collectives  332 us (53%)
  waiting for transfers between devices  182 us (29%)
  other arithmetic  67.8 us (11%)
  matrix products  25.5 us (4%)
  between operations  13.5 us (2%)
    pmax x2, blocking collectives, row_norm(): peak = lax.pmax(jnp.max(shifted, axis=1), 'cent')  142 us
    psum x2, blocking collectives, row_norm(): total = lax.psum(jnp.sum(jnp.exp(shifted - peak[:, None]), axis=1), 'cent')  127 us
    psum x1, waiting for transfers between devices, shards(): total_sums, total_mass = lax.psum((sums, mass), 'dp')  125 us
    all_gather x1, waiting for transfers between devices, shards(): docs = lax.all_gather(embeddings, 'cent', axis=0, tiled=True)  56.9 us
    pmax x2, blocking collectives, col_norm(): peak = lax.pmax(jnp.max(shifted, axis=0), 'dp')  26 us
    psum x2, blocking collectives, col_norm(): total = lax.psum(jnp.sum(jnp.exp(shifted - peak[None, :]), axis=0), 'dp')  23.4 us
    reduce_sum x2, other arithmetic, col_norm(): total = lax.psum(jnp.sum(jnp.exp(shifted - peak[None, :]), axis=0), 'dp')  16.5 us
    reduce_sum x2, other arithmetic, row_norm(): total = lax.psum(jnp.sum(jnp.exp(shifted - peak[:, None]), axis=1), 'cent')  15.9 us
  transfers between devices with their start and end apart: 2, of which 2 were waited for; matrix products, arithmetic and copies ran while one was open for 1% of the time, Pallas kernels for 0%

commit v1 on v0

v1 whole, which is shorter than its diff:
```python
import functools
import math

import jax
import jax.numpy as jnp
from jax import lax
from jax.experimental import pallas as pl
from jax.experimental.pallas import tpu as pltpu
from jax.sharding import PartitionSpec as P

f32 = jnp.float32
bf16 = jnp.bfloat16
LANES = 128
BLOCK = 256
CHUNK = 16
SCALE = 3.0
SMALL_SUM = 1e-20
LARGE_POT = 46.0
NT = (((1,), (1,)), ((), ()))


def eye():
    rows = lax.broadcasted_iota(jnp.int32, (LANES, LANES), 0)
    cols = lax.broadcasted_iota(jnp.int32, (LANES, LANES), 1)
    return rows == cols


def to_row(column):
    return jnp.sum(jnp.where(eye(), column, 0.0), axis=0, keepdims=True)


def to_column(row):
    return jnp.sum(jnp.where(eye(), row, 0.0), axis=1, keepdims=True)


def fold(x, op):
    out = x[:, :LANES]
    for at in range(LANES, x.shape[1], LANES):
        out = op(out, x[:, at : at + LANES])
    return out


def merge(parts):
    peak = jnp.max(parts, axis=0)
    return peak + jnp.log(jnp.sum(jnp.exp(parts - peak[None]), axis=0))


def logits_block(cents, docs_ref, out_ref, rows):
    width = 512
    for at in range(0, docs_ref.shape[0], width):
        out_ref[rows, at : at + width] = lax.dot_general(
            cents, docs_ref[at : at + width, :], NT, preferred_element_type=f32
        )


def first_kernel(docs_ref, cents_ref, t_ref, peak_ref, lse_ref, wide_peak, wide_lse):
    n_cent = cents_ref.shape[0]

    def block(t, _):
        start = pl.multiple_of(t * BLOCK, BLOCK)
        rows = pl.ds(start, BLOCK)
        logits_block(cents_ref[rows, :], docs_ref, t_ref, rows)
        for c in range(BLOCK // CHUNK):
            at = pl.ds(start + c * CHUNK, CHUNK)
            x = t_ref[at, :]
            peak = jnp.max(fold(x, jnp.maximum), axis=1, keepdims=True)
            e = jnp.exp((x - peak) * SCALE)
            t_ref[at, :] = e
            total = jnp.sum(fold(e, jnp.add), axis=1, keepdims=True)
            peak = jnp.broadcast_to(peak * SCALE, (CHUNK, LANES))
            wide_peak[at, :] = peak
            wide_lse[at, :] = peak + jnp.log(jnp.broadcast_to(total, (CHUNK, LANES)))
        return 0

    lax.fori_loop(0, n_cent // BLOCK, block, 0)
    for b in range(n_cent // LANES):
        at = slice(b * LANES, (b + 1) * LANES)
        peak_ref[b : b + 1, :] = to_row(wide_peak[at, :])
        lse_ref[:, b, :] = jnp.broadcast_to(to_row(wide_lse[at, :]), (lse_ref.shape[0], LANES))


def load_all(docs_hbm, cents_hbm, docs, cents):
    pltpu.sync_copy(docs_hbm, docs)
    pltpu.sync_copy(cents_hbm, cents)


def row_slow(docs_hbm, cents_hbm, col_wide, lse_ref):
    n_doc, n_cent = docs_hbm.shape[0], cents_hbm.shape[0]

    def body(docs, cents, x_ref, peak, total):
        load_all(docs_hbm, cents_hbm, docs, cents)
        peak[...] = jnp.full(peak.shape, -jnp.inf, f32)
        total[...] = jnp.zeros(total.shape, f32)

        def sweep(last):
            def block(t, _):
                start = pl.multiple_of(t * BLOCK, BLOCK)
                rows = pl.ds(start, BLOCK)
                logits_block(cents[rows, :], docs, x_ref, pl.ds(0, BLOCK))
                for at in range(0, n_doc, LANES):
                    y = x_ref[:, at : at + LANES] * SCALE + col_wide[rows, :]
                    here = peak[:, at : at + LANES]
                    if last:
                        total[:, at : at + LANES] += jnp.sum(jnp.exp(y - here), axis=0, keepdims=True)
                    else:
                        peak[:, at : at + LANES] = jnp.maximum(here, jnp.max(y, axis=0, keepdims=True))
                return 0

            lax.fori_loop(0, n_cent // BLOCK, block, 0)

        sweep(False)
        sweep(True)
        for b in range(n_doc // LANES):
            at = slice(b * LANES, (b + 1) * LANES)
            value = peak[:, at] + jnp.log(total[:, at])
            lse_ref[:, b, :] = jnp.broadcast_to(value, (lse_ref.shape[0], LANES))

    pl.run_scoped(
        body,
        pltpu.VMEM(docs_hbm.shape, bf16),
        pltpu.VMEM(cents_hbm.shape, bf16),
        pltpu.VMEM((BLOCK, n_doc), f32),
        pltpu.VMEM((1, n_doc), f32),
        pltpu.VMEM((1, n_doc), f32),
    )


def row_kernel(log_ratio, t_ref, peak_ref, parts_ref, docs_hbm, cents_hbm, lse_ref, col_ref, wide, acc):
    n_cent, n_doc = t_ref.shape
    col = log_ratio - merge(parts_ref[...])
    col_ref[...] = col
    factor = jnp.exp(peak_ref[...] + col)
    for b in range(n_cent // LANES):
        column = to_column(factor[b : b + 1, :])
        wide[b * LANES : (b + 1) * LANES, :] = jnp.broadcast_to(column, (LANES, LANES))
    acc[...] = jnp.zeros(acc.shape, f32)
    step = 64

    def block(t, _):
        start = pl.multiple_of(t * step, step)
        scale = wide[pl.ds(start, step), :]
        for at in range(0, n_doc, LANES):
            x = t_ref[pl.ds(start, step), at : at + LANES] * scale
            part = x[:8, :]
            for r in range(8, step, 8):
                part = part + x[r : r + 8, :]
            acc[:, at : at + LANES] += part
        return 0

    lax.fori_loop(0, n_cent // step, block, 0)
    least = jnp.full((1, LANES), jnp.inf, f32)
    for b in range(n_doc // LANES):
        total = jnp.sum(acc[:, b * LANES : (b + 1) * LANES], axis=0, keepdims=True)
        least = jnp.minimum(least, total)
        lse_ref[:, b, :] = jnp.broadcast_to(jnp.log(total), (lse_ref.shape[0], LANES))

    @pl.when(jnp.logical_not(jnp.min(least) >= SMALL_SUM))
    def _():
        for b in range(n_cent // LANES):
            column = to_column(col[b : b + 1, :])
            wide[b * LANES : (b + 1) * LANES, :] = jnp.broadcast_to(column, (LANES, LANES))
        row_slow(docs_hbm, cents_hbm, wide, lse_ref)


def col_slow(docs_hbm, cents_hbm, row_pot, wide_lse):
    n_doc, n_cent = docs_hbm.shape[0], cents_hbm.shape[0]

    def body(docs, cents, x_ref):
        load_all(docs_hbm, cents_hbm, docs, cents)

        def block(t, _):
            start = pl.multiple_of(t * BLOCK, BLOCK)
            logits_block(cents[pl.ds(start, BLOCK), :], docs, x_ref, pl.ds(0, BLOCK))

            def chunk(c, _):
                at = pl.multiple_of(c * CHUNK, CHUNK)
                y = [
                    x_ref[pl.ds(at, CHUNK), b * LANES : (b + 1) * LANES] * SCALE + row_pot[b : b + 1, :]
                    for b in range(n_doc // LANES)
                ]
                peak = jnp.max(functools.reduce(jnp.maximum, y), axis=1, keepdims=True)
                total = jnp.sum(sum(jnp.exp(part - peak) for part in y), axis=1, keepdims=True)
                value = peak + jnp.log(total)
                wide_lse[pl.ds(start + at, CHUNK), :] = jnp.broadcast_to(value, (CHUNK, LANES))
                return 0

            return lax.fori_loop(0, BLOCK // CHUNK, chunk, 0)

        lax.fori_loop(0, n_cent // BLOCK, block, 0)

    pl.run_scoped(
        body,
        pltpu.VMEM(docs_hbm.shape, bf16),
        pltpu.VMEM(cents_hbm.shape, bf16),
        pltpu.VMEM((BLOCK, n_doc), f32),
    )


def col_kernel(t_ref, peak_ref, parts_ref, docs_hbm, cents_hbm, lse_ref, wide_lse):
    n_cent, n_doc = t_ref.shape
    row_pot = -merge(parts_ref[...])
    factor = jnp.exp(row_pot)
    step = 64

    def block(t, _):
        start = pl.multiple_of(t * step, step)
        total = jnp.zeros((step, LANES), f32)
        for b in range(n_doc // LANES):
            total = total + t_ref[pl.ds(start, step), b * LANES : (b + 1) * LANES] * factor[b : b + 1, :]
        total = jnp.sum(total, axis=1, keepdims=True)
        wide_lse[pl.ds(start, step), :] = jnp.log(jnp.broadcast_to(total, (step, LANES)))
        return 0

    lax.fori_loop(0, n_cent // step, block, 0)
    good = jnp.max(row_pot) <= LARGE_POT
    for b in range(n_cent // LANES):
        at = slice(b * LANES, (b + 1) * LANES)
        value = to_row(wide_lse[at, :]) + peak_ref[b : b + 1, :]
        lse_ref[:, b, :] = jnp.broadcast_to(value, (lse_ref.shape[0], LANES))

    @pl.when(jnp.logical_not(good))
    def _():
        def body(pot):
            pot[...] = row_pot
            col_slow(docs_hbm, cents_hbm, pot, wide_lse)

        pl.run_scoped(body, pltpu.VMEM(row_pot.shape, f32))
        for b in range(n_cent // LANES):
            value = to_row(wide_lse[b * LANES : (b + 1) * LANES, :])
            lse_ref[:, b, :] = jnp.broadcast_to(value, (lse_ref.shape[0], LANES))


def last_kernel(t_ref, peak_ref, col_ref, parts_ref, docs_ref, cents_hbm, sums_ref, mass_ref, wide, wide_mass, pot, plan):
    n_cent, n_doc = t_ref.shape
    row_pot = -merge(parts_ref[...])
    good = jnp.max(row_pot) <= LARGE_POT
    pot[...] = jnp.where(good, jnp.exp(row_pot), row_pot)
    by_col = jnp.where(good, jnp.exp(peak_ref[...] + col_ref[...]), col_ref[...])
    for b in range(n_cent // LANES):
        column = to_column(by_col[b : b + 1, :])
        wide[b * LANES : (b + 1) * LANES, :] = jnp.broadcast_to(column, (LANES, LANES))

    def finish(start):
        mass = None
        for b in range(n_doc // LANES):
            part = fold(plan[:, b * LANES : (b + 1) * LANES].astype(f32), jnp.add)
            mass = part if mass is None else mass + part
        mass = jnp.sum(mass, axis=1, keepdims=True)
        wide_mass[pl.ds(start, BLOCK), :] = jnp.broadcast_to(mass, (BLOCK, LANES))
        sums_ref[pl.ds(start, BLOCK), :] = jnp.dot(plan[...], docs_ref[...], preferred_element_type=f32)

    @pl.when(good)
    def _():
        def block(t, _):
            start = pl.multiple_of(t * BLOCK, BLOCK)
            scale = wide[pl.ds(start, BLOCK), :]
            for b in range(n_doc // LANES):
                at = slice(b * LANES, (b + 1) * LANES)
                plan[:, at] = (t_ref[pl.ds(start, BLOCK), at] * scale * pot[b : b + 1, :]).astype(bf16)
            finish(start)
            return 0

        lax.fori_loop(0, n_cent // BLOCK, block, 0)

    @pl.when(jnp.logical_not(good))
    def _():
        def body(cents, x_ref):
            pltpu.sync_copy(cents_hbm, cents)

            def block(t, _):
                start = pl.multiple_of(t * BLOCK, BLOCK)
                logits_block(cents[pl.ds(start, BLOCK), :], docs_ref, x_ref, pl.ds(0, BLOCK))
                col = wide[pl.ds(start, BLOCK), :]
                for b in range(n_doc // LANES):
                    at = slice(b * LANES, (b + 1) * LANES)
                    plan[:, at] = jnp.exp(x_ref[:, at] * SCALE + pot[b : b + 1, :] + col).astype(bf16)
                finish(start)
                return 0

            lax.fori_loop(0, n_cent // BLOCK, block, 0)

        pl.run_scoped(body, pltpu.VMEM(cents_hbm.shape, bf16), pltpu.VMEM((BLOCK, n_doc), f32))

    for b in range(n_cent // LANES):
        mass_ref[b : b + 1, :] = to_row(wide_mass[b * LANES : (b + 1) * LANES, :])


def divide_kernel(sums_ref, mass_ref, out_ref):
    mass = jnp.sum(mass_ref[...], axis=0)
    for b in range(mass.shape[0]):
        at = slice(b * LANES, (b + 1) * LANES)
        out_ref[at, :] = (sums_ref[at, :] / to_column(mass[b : b + 1, :])).astype(bf16)


IN_VMEM = pl.BlockSpec(memory_space=pltpu.VMEM)
IN_HBM = pl.BlockSpec(memory_space=pl.ANY)


def params(mib):
    return pltpu.CompilerParams(vmem_limit_bytes=mib * 2**20)


def shards(embeddings, centroids):
    groups, blocks = lax.axis_size("dp"), lax.axis_size("cent")
    docs = lax.all_gather(embeddings, "cent", axis=0, tiled=True)
    n_doc, depth = docs.shape
    n_cent = centroids.shape[0]
    log_ratio = math.log(n_doc * groups / (n_cent * blocks))
    row_shape = (n_doc // LANES, LANES)
    col_shape = (n_cent // LANES, LANES)
    shaped = jax.ShapeDtypeStruct
    by_group = shaped((groups, *col_shape), f32)
    by_block = shaped((blocks, *row_shape), f32)
    wide = pltpu.VMEM((n_cent, LANES), f32)

    t, peak, lse = pl.pallas_call(
        first_kernel,
        out_shape=(pltpu.VMEM((n_cent, n_doc), f32), shaped(col_shape, f32), by_group),
        in_specs=[IN_VMEM, IN_VMEM],
        out_specs=(IN_VMEM, IN_VMEM, IN_VMEM),
        scratch_shapes=[wide, wide],
        compiler_params=params(20),
    )(docs, centroids)

    def rows(lse):
        parts = lax.all_to_all(lse, "dp", 0, 0)
        return pl.pallas_call(
            functools.partial(row_kernel, log_ratio),
            out_shape=(by_block, shaped(col_shape, f32)),
            in_specs=[IN_VMEM, IN_VMEM, IN_VMEM, IN_HBM, IN_HBM],
            out_specs=(IN_VMEM, IN_VMEM),
            scratch_shapes=[wide, pltpu.VMEM((8, n_doc), f32)],
            compiler_params=params(20),
        )(t, peak, parts, docs, centroids)

    def cols(lse):
        parts = lax.all_to_all(lse, "cent", 0, 0)
        return pl.pallas_call(
            col_kernel,
            out_shape=by_group,
            in_specs=[IN_VMEM, IN_VMEM, IN_VMEM, IN_HBM, IN_HBM],
            out_specs=IN_VMEM,
            scratch_shapes=[wide],
            compiler_params=params(20),
        )(t, peak, parts, docs, centroids)

    lse, _ = rows(lse)
    lse = cols(lse)
    lse, col = rows(lse)
    parts = lax.all_to_all(lse, "cent", 0, 0)
    sums, mass = pl.pallas_call(
        last_kernel,
        out_shape=(shaped((n_cent, depth), f32), shaped(col_shape, f32)),
        in_specs=[IN_VMEM, IN_VMEM, IN_VMEM, IN_VMEM, IN_VMEM, IN_HBM],
        out_specs=(IN_VMEM, IN_VMEM),
        scratch_shapes=[wide, wide, pltpu.VMEM(row_shape, f32), pltpu.VMEM((BLOCK, n_doc), bf16)],
        compiler_params=params(30),
    )(t, peak, col, parts, docs, centroids)
    sums = lax.psum_scatter(sums, "dp", scatter_dimension=0, tiled=True)
    mass = lax.all_to_all(mass.reshape(groups, n_cent // groups // LANES, LANES), "dp", 0, 0)
    new = pl.pallas_call(
        divide_kernel,
        out_shape=shaped(sums.shape, bf16),
        in_specs=[IN_VMEM, IN_VMEM],
        out_specs=IN_VMEM,
    )(sums, mass)
    return lax.all_gather(new, "dp", axis=0, tiled=True)


def solution(mesh):
    placed = (P(("dp", "cent"), None), P("cent", None))
    return jax.shard_map(
        shards, mesh=mesh, in_specs=placed, out_specs=P("cent", None), check_vma=False
    )
```

time: 625 us -> 296 us (0.47)
  blocking collectives: 332 us -> 62 us
  other arithmetic: 67.8 us -> 0 us
  Pallas kernels: 0 us -> 51 us
  matrix products: 25.5 us -> 0 us
  waiting for transfers between devices: 182 us -> 159 us
  local copies, waits for them, and re-layouts: 3.22 us -> 10.2 us
    pmax x4 -> x0, blocking collectives: 168 us -> none  [the longest x2 142 us: row_norm(): peak = lax.pmax(jnp.max(shifted, axis=1), 'cent')]
    psum x5 -> x0, blocking collectives: 165 us -> none  [the longest x2 127 us: row_norm(): total = lax.psum(jnp.sum(jnp.exp(shifted - peak[:, None]), axis=1), 'cent')]
    psum x1 -> x0, waiting for transfers between devices: 125 us -> none  [shards(): total_sums, total_mass = lax.psum((sums, mass), 'dp')]
    all_to_all x0 -> x5, blocking collectives: none -> 62 us  [the longest x2 23.3 us: rows(): parts = lax.all_to_all(lse, 'dp', 0, 0)]
    reduce_scatter x0 -> x1, waiting for transfers between devices: none -> 58.1 us  [shards(): sums = lax.psum_scatter(sums, 'dp', scatter_dimension=0, tiled=True)]
    pallas_call x0 -> x6, Pallas kernels: none -> 51 us  [the longest x1 23.7 us: shards(): pl.pallas_call(first_kernel, out_shape=(pltpu.VMEM((n_cent, n_doc), f32),...]
    all_gather x0 -> x1, waiting for transfers between devices: none -> 43.3 us  [shards(): return lax.all_gather(new, 'dp', axis=0, tiled=True)]
    reduce_sum x4 -> x0, other arithmetic: 32.5 us -> none  [the longest x2 16.5 us: col_norm(): total = lax.psum(jnp.sum(jnp.exp(shifted - peak[None, :]), axis=0), 'dp')]
  transfers between devices with their start and end apart: 2 -> 3, of which waited for: 2 -> 3; matrix products, arithmetic and copies ran while one was open for 1% -> 0% of each run, Pallas kernels for 0% -> 0%
where the time goes in v1:
time: 296 us
  waiting for transfers between devices  159 us (54%)
  blocking collectives  62 us (21%)
  Pallas kernels  51 us (17%)
  between operations  13.2 us (4%)
  local copies, waits for them, and re-layouts  10.2 us (3%)
    reduce_scatter x1, waiting for transfers between devices, shards(): sums = lax.psum_scatter(sums, 'dp', scatter_dimension=0, tiled=True)  58.1 us
    all_gather x1, waiting for transfers between devices, shards(): docs = lax.all_gather(embeddings, 'cent', axis=0, tiled=True)  56.9 us
    all_gather x1, waiting for transfers between devices, shards(): return lax.all_gather(new, 'dp', axis=0, tiled=True)  43.3 us
    pallas_call x1, Pallas kernels, shards(): pl.pallas_call(first_kernel, out_shape=(pltpu.VMEM((n_cent, n_doc), f32),...  23.7 us
    all_to_all x2, blocking collectives, rows(): parts = lax.all_to_all(lse, 'dp', 0, 0)  23.3 us
    pallas_call x1, Pallas kernels, shards(): pl.pallas_call(last_kernel, out_shape=(shaped((n_cent, depth), f32), shap...  16.2 us
    all_to_all x1, blocking collectives, cols(): parts = lax.all_to_all(lse, 'cent', 0, 0)  15.4 us
    all_to_all x1, blocking collectives, shards(): parts = lax.all_to_all(lse, 'cent', 0, 0)  13.7 us
  transfers between devices with their start and end apart: 3, of which 3 were waited for; matrix products, arithmetic and copies ran while one was open for 0% of the time, Pallas kernels for 0%

profile of v1, /device:TPU:1, one launch (start us, length us, event | category | flops | bytes accessed | tf_op | source)
XLA Modules:
  0.0 295.5 jit_solution(16433228745657953788)
XLA Ops:
  6.5 0.0 all-gather.3.cloned.1.call-start
  6.5 0.7 all-gather.3.cloned.1.call-update
  7.3 0.0 reduce-scatter.2.cloned.1.call-start
  7.3 56.9 %all-gather.3.cloned.1.call-done.docs_ref.docs_hbm = bf16[2048,768]{1,0:T(8,128)(2,1)} async-done(((bf16[64,768]{1,0:T(8,128)(2,1)}), bf16[2048,768]{1,0:T(8,128)(2,1)}) %all-gather.3.cloned.1.call-update) | async-done | bytes 3145744 | tf_op jit(solution)/shard_map/all_gather | solution.py:305
  64.2 0.0 copy-start.1
  64.2 1.9 copy-done.1
  66.1 0.0 copy-start.3
  66.1 1.9 copy-done.3
  68.0 23.7 %shard_map.28 = (f32[2048,2048]{1,0:T(8,128)S(1)}, f32[16,128]{1,0:T(8,128)S(1)}, f32[8,16,128]{2,1,0:T(8,128)S(1)}) custom-call(bf16[2048,768]{1,0:T(8,128)(2,1)S(1)} %copy-done.3, bf16[2048,768]{1,0:T(8,128)(2,1)S(1)} %copy-done.1), custom_call_target="tpu_custom_call" | custom-call | tf_op jit(solution)/shard_map/pallas_call | solution.py:316
  91.7 0.0 copy-start
  91.7 13.8 %all_to_all.25.parts_ref = f32[8,16,128]{2,1,0:T(8,128)S(1)} all-to-all(f32[8,16,128]{2,1,0:T(8,128)S(1)} %get-tuple-element.15), channel_id=1, replica_groups=mesh['dp'=8,'cent'=32] {'dp'}, dimensions={0} | all-to-all | bytes 131072 | tf_op jit(solution)/shard_map/all_to_all | solution.py:326
  105.5 2.7 shard_map.29
  108.2 15.4 %all_to_all.26.parts_ref = f32[32,16,128]{2,1,0:T(8,128)S(1)} all-to-all(f32[32,16,128]{2,1,0:T(8,128)S(1)} %get-tuple-element.16), channel_id=1, replica_groups=mesh['dp'=8,'cent'=32] {'cent'}, dimensions={0} | all-to-all | bytes 524288 | tf_op jit(solution)/shard_map/all_to_all | solution.py:337
  123.6 4.2 %shard_map.30 = f32[8,16,128]{2,1,0:T(8,128)S(1)} custom-call(f32[2048,2048]{1,0:T(8,128)S(1)} %get-tuple-element.13.t_ref, f32[16,128]{1,0:T(8,128)S(1)} %get-tuple-element.14.peak_ref, f32[32,16,128]{2,1,0:T(8,128)S(1)} %all_to_all.26.parts_ref, bf16[2048,768]{1,0:T(8,128)(2,1)S(1)} %copy-done.3, bf16[2048,768]{1,0:T(8,128)(2,1)S(1)} %copy-done.1), custom_call_target="tpu_custom_call" | custom-call | tf_op jit(solution)/shard_map/pallas_call | solution.py:338
  127.8 9.5 %all_to_all.27.parts_ref = f32[8,16,128]{2,1,0:T(8,128)S(1)} all-to-all(f32[8,16,128]{2,1,0:T(8,128)S(1)} %shard_map.30), channel_id=1, replica_groups=mesh['dp'=8,'cent'=32] {'dp'}, dimensions={0} | all-to-all | bytes 131072 | tf_op jit(solution)/shard_map/all_to_all | solution.py:326
  137.4 0.0 copy-done
  137.4 0.0 copy-start.2
  137.4 0.0 copy-start.4
  137.4 2.1 shard_map.31
  139.5 13.7 %all_to_all.28.parts_ref = f32[32,16,128]{2,1,0:T(8,128)S(1)} all-to-all(f32[32,16,128]{2,1,0:T(8,128)S(1)} %get-tuple-element.18), channel_id=1, replica_groups=mesh['dp'=8,'cent'=32] {'cent'}, dimensions={0} | all-to-all | bytes 524288 | tf_op jit(solution)/shard_map/all_to_all | solution.py:350
  153.2 0.0 copy-done.2
  153.2 0.0 copy-done.4
  153.2 16.2 %shard_map.32 = (f32[2048,768]{1,0:T(8,128)S(1)}, f32[16,128]{1,0:T(8,128)S(1)}) custom-call(f32[2048,2048]{1,0:T(8,128)} %copy-done, f32[16,128]{1,0:T(8,128)S(1)} %get-tuple-element.14.peak_ref, f32[16,128]{1,0:T(8,128)S(1)} %get-tuple-element.17.col_ref, f32[32,16,128]{2,1,0:T(8,128)S(1)} %all_to_all.28.parts_ref, bf16[2048,768]{1,0:T(8,128)(2,1)S(1)} %copy-done.4, ...), custom_call_target="tpu_custom_call" | custom-call | tf_op jit(solution)/shard_map/pallas_call | solution.py:351
  169.4 0.0 copy-start.5
  169.4 2.7 copy-done.5
  172.1 0.0 reduce-scatter.2.cloned.1.call-update
  172.1 0.0 all-gather.5.cloned.1.call-start
  172.1 9.7 %all_to_all.29.mass_ref = f32[8,2,128]{2,1,0:T(2,128)} all-to-all(f32[8,2,128]{2,1,0:T(2,128)S(1)} %bitcast.1), channel_id=1, replica_groups=mesh['dp'=8,'cent'=32] {'dp'}, dimensions={0} | all-to-all | bytes 16384 | tf_op jit(solution)/shard_map/all_to_all | solution.py:360
  181.8 58.1 %reduce-scatter.2.cloned.1.call-done.sums_ref = f32[256,768]{1,0:T(8,128)} async-done(((f32[2048,768]{1,0:T(8,128)}), f32[256,768]{1,0:T(8,128)}) %reduce-scatter.2.cloned.1.call-update) | async-done | bytes 786448 | tf_op jit(solution)/shard_map/reduce_scatter | solution.py:359
  239.9 2.0 shard_map.33
  242.0 0.0 all-gather.5.cloned.1.call-update
  242.0 43.3 %all-gather.5.cloned.1.call-done = bf16[2048,768]{1,0:T(8,128)(2,1)} async-done(((bf16[256,768]{1,0:T(8,128)(2,1)}), bf16[2048,768]{1,0:T(8,128)(2,1)}) %all-gather.5.cloned.1.call-update) | async-done | bytes 3145744 | tf_op jit(solution)/shard_map/all_gather | solution.py:367
  285.3 3.8 %copy.4 = bf16[2048,768]{1,0:T(8,128)(2,1)} copy(bf16[2048,768]{1,0:T(8,128)(2,1)} %all-gather.5.cloned.1.call-done) | data formatting | bytes 6291456
Async XLA Ops:
  6.5 57.7 %all-gather.3.cloned.1.call-start = ((), (), s32[]{:S(2)}) async-start(), calls=%async_computation.6 | async-start | bytes 3244032 | tf_op jit(solution)/shard_map/all_gather | solution.py:305
  7.3 232.7 %reduce-scatter.2.cloned.1.call-start = ((), (), s32[]{:S(2)}) async-start(), calls=%async_computation.7 | async-start | bytes 7077888 | tf_op jit(solution)/shard_map/reduce_scatter | solution.py:359
  64.2 1.9 copy-start.1
  66.1 1.9 copy-start.3
  91.7 45.6 %copy-start = (f32[2048,2048]{1,0:T(8,128)}, f32[2048,2048]{1,0:T(8,128)S(1)}, u32[]{:S(2)}) copy-start(f32[2048,2048]{1,0:T(8,128)S(1)} %get-tuple-element.13.t_ref) | copy-start | bytes 50331652
  137.4 15.8 %copy-start.2 = (bf16[2048,768]{1,0:T(8,128)(2,1)S(1)}, bf16[2048,768]{1,0:T(8,128)(2,1)}, u32[]{:S(2)}) copy-start(bf16[2048,768]{1,0:T(8,128)(2,1)} %cents_hbm.7) | copy-start | bytes 9437188
  137.4 15.8 %copy-start.4 = (bf16[2048,768]{1,0:T(8,128)(2,1)S(1)}, bf16[2048,768]{1,0:T(8,128)(2,1)}, u32[]{:S(2)}) copy-start(bf16[2048,768]{1,0:T(8,128)(2,1)} %all-gather.3.cloned.1.call-done.docs_ref.docs_hbm) | copy-start | bytes 9437188
  169.4 2.7 copy-start.5
  172.1 113.2 %all-gather.5.cloned.1.call-start = ((), (), s32[]{:S(2)}) async-start(), calls=%async_computation.8 | async-start | bytes 3538944 | tf_op jit(solution)/shard_map/all_gather | solution.py:367
Sparse Core Ops, SparseCore 0:
  9.9 54.2 all-gather.2
  172.2 67.6 reduce-scatter.1
  242.1 43.1 all-gather.4
